TPU v7x, 32 devices: a whole 2x2x4 slice. The times are simulated.
32 devices in a mesh: groups: 2 (over y), tensor: 4 (over z), replica: 4 (over x, core).
Axes of the slice: x: 2, y: 2, z: 4, core: 2. Of those that a mesh axis runs over, the one named last changes fastest.
Arguments:
- hidden: bfloat16 [32, 2, 8192], P(('groups', 'replica')), parts along dimension 0, may hold values from -32 to 32
- query: bfloat16 [32, 2, 512], P(('groups', 'replica'), None, 'tensor'), parts along dimension 0, may hold values from -96 to 96
- incoming_key_value: bfloat16 [32, 2, 4, 256], P(('groups', 'replica'), None, 'tensor'), parts along dimension 0, may hold values from -4 to 4, as said below
- cache: bfloat16 [32, 256, 4, 256], P(('groups', 'replica'), None, 'tensor'), parts along dimension 0, may hold values from -4 to 4, as said below
- lengths: int32 [32], P(('groups', 'replica')), parts along dimension 0, may hold values from 2 to 256, as said below
- output_projection_weight: bfloat16 [512, 8192], P('tensor'), may hold values from -0.25 to 0.25
- adapter_down_factor: bfloat16 [128, 512], P(('groups', 'tensor')), parts along dimension 0, may hold values from -0.25 to 0.25
- adapter_up_factor: bfloat16 [16384, 64], P(('groups', 'tensor', 'replica')), parts along dimension 0, may hold values from -0.75 to 0.75
- gain: float32 [8192], replicated, may hold values from 0.1 to 1.9
Outputs:
- normed: bfloat16 [32, 2, 8192], P(('groups', 'replica')), parts along dimension 0
- merged: bfloat16 [1024, 8192], P(('groups', 'tensor')), parts along dimension 0
There are 2 independent parts, one for each index of `groups`. A program takes and returns all parts, laid end to end along the dimension named above; an argument that names none is the same for every part. Nothing has to cross between parts.
Inputs may be any that keep to these rules, and one draw needn't show every extreme that they name: `cache`: the slots of the 1 consecutive query heads of one group are equal. `incoming_key_value`: the slots of the 1 consecutive query heads of one group are equal. `lengths`: some row has exactly 256.
All inputs are finite; a program needn't handle non-finite values.
Results may differ from a plain program's by a relative error of at most 0.0052.
Values may be sent and summed in bfloat16 or wider, within the bound.
A program may use at most 64 MiB of HBM per device.

v0:
```python
import math

import jax
import jax.numpy as jnp
from jax import lax
from jax.sharding import PartitionSpec as P

HEAD_SIZE = 128


ADAPTER_SCALE = 2.0
EPS = 1e-06


def attend(query, incoming_key_value, cache, lengths):
    row_count, steps, features = query.shape
    heads = features // HEAD_SIZE
    span = cache.shape[1]
    queries = query.reshape(row_count, steps, heads, HEAD_SIZE)
    scale_factor = 1.0 / math.sqrt(HEAD_SIZE)
    older = (
        jnp.einsum(
            "rihd,rlhd->rihl", queries, cache[..., :HEAD_SIZE], preferred_element_type=jnp.float32
        )
        * scale_factor
    )
    fresh = (
        jnp.einsum(
            "rihd,rjhd->rihj",
            queries,
            incoming_key_value[..., :HEAD_SIZE],
            preferred_element_type=jnp.float32,
        )
        * scale_factor
    )
    live_old = jnp.arange(span, dtype=jnp.int32)[None, None, None, :] < lengths[:, None, None, None]
    live_new = (
        jnp.arange(steps, dtype=jnp.int32)[None, None, None, :]
        <= jnp.arange(steps, dtype=jnp.int32)[None, :, None, None]
    )
    scores = jnp.concatenate(
        [jnp.where(live_old, older, -1e30), jnp.where(live_new, fresh, -1e30)], axis=3
    )
    weights = jax.nn.softmax(scores, axis=3).astype(jnp.bfloat16)
    mixed = jnp.einsum(
        "rihl,rlhd->rihd",
        weights[..., :span],
        cache[..., HEAD_SIZE:],
        preferred_element_type=jnp.float32,
    )
    mixed = mixed + jnp.einsum(
        "rihj,rjhd->rihd",
        weights[..., span:],
        incoming_key_value[..., HEAD_SIZE:],
        preferred_element_type=jnp.float32,
    )
    return mixed.astype(jnp.bfloat16).reshape(row_count, steps, features)


def per_device(
    hidden,
    query,
    incoming_key_value,
    cache,
    lengths,
    output_projection_weight,
    adapter_down_factor,
    adapter_up_factor,
    gain,
):
    context = attend(query, incoming_key_value, cache, lengths)
    owned = output_projection_weight.shape[0]
    complete_down_factor = lax.all_gather(adapter_down_factor, "tensor", axis=0, tiled=True)
    a_columns = lax.dynamic_slice_in_dim(
        complete_down_factor, lax.axis_index("tensor") * owned, owned, 1
    )
    adapter_update = lax.dot_general(
        a_columns,
        lax.all_gather(adapter_up_factor, ("tensor", "replica"), axis=0, tiled=True),
        (((0,), (1,)), ((), ())),
        preferred_element_type=jnp.float32,
    )
    merged = (output_projection_weight.astype(jnp.float32) + ADAPTER_SCALE * adapter_update).astype(
        jnp.bfloat16
    )
    row_count, steps = (context.shape[0], context.shape[1])
    partial_value = jnp.dot(
        context.reshape(row_count * steps, owned), merged, preferred_element_type=jnp.float32
    )
    partial_value = partial_value.reshape(row_count, steps, merged.shape[1])
    summed = lax.psum(partial_value, "tensor")
    resid = hidden.astype(jnp.float32) + summed
    mean_square = jnp.mean(resid * resid, axis=-1, keepdims=True)
    normed = (resid * lax.rsqrt(mean_square + EPS) * gain).astype(jnp.bfloat16)
    return (normed, merged)


def solution(mesh):
    return jax.shard_map(
        per_device,
        mesh=mesh,
        in_specs=(
            P(("groups", "replica"), None, None),
            P(("groups", "replica"), None, "tensor"),
            P(("groups", "replica"), None, "tensor", None),
            P(("groups", "replica"), None, "tensor", None),
            P(("groups", "replica")),
            P("tensor", None),
            P(("groups", "tensor"), None),
            P(("groups", "tensor", "replica"), None),
            P(),
        ),
        out_specs=(P(("groups", "replica"), None, None), P(("groups", "tensor"), None)),
        check_vma=False,
    )
```

profile of v0, /device:TPU:0, one launch (start us, length us, event | category | flops | bytes accessed | tf_op | source)
XLA Modules:
  0.0 98.8 jit_solution(17614123657421967939)
XLA Ops:
  7.2 0.0 copy-start
  7.2 0.0 all-gather.2.cloned.1.call-start
  7.2 0.7 all-gather.2.cloned.1.call-update
  7.9 0.0 all-reduce.2.cloned.1.call-start
  8.0 0.7 iota_compare_fusion
  8.7 0.9 fusion.20
  9.6 1.2 %fusion.19 = (f32[4,2]{1,0:T(4,128)S(1)}, f32[4,2,1,256]{3,1,0,2:T(2,128)S(1)}) fusion(bf16[4,2,128]{2,1,0:T(2,128)(2,1)S(1)} %copy-done, bf16[4,256,1,256]{3,1,0,2:T(8,128)(2,1)} %bitcast.44, pred[4,256]{1,0:T(4,128)(4,1)S(1)} %iota_compare_fusion), kind=kOutput, calls=%fused_computation.35 | convolution fusion | flops 530424 | bytes 273440 | tf_op jit(solution)/shard_map/rihd,rlhd->rihl/dot_general | solution.py:22
  10.8 15.2 %all_gather.6 = bf16[64,512]{1,0:T(8,128)(2,1)S(1)} all-gather(bf16[16,512]{1,0:T(8,128)(2,1)} %param.15), channel_id=1, replica_groups=mesh['groups'=2,'tensor'=4,'replica'=4] {'tensor'}, dimensions={0}, use_global_device_ids=true | all-gather | bytes 81920 | tf_op jit(solution)/shard_map/all_gather | solution.py:73
  26.0 0.2 fusion.18
  26.1 0.1 divide_convert_fusion
  26.2 0.8 fusion.16
  27.0 1.1 %fusion.9 = f32[4,2,128]{2,1,0:T(2,128)S(1)} fusion(bf16[4,256,1,256]{3,1,2,0:T(8,128)(2,1)} %param.12, bf16[4,2,1,258]{3,1,0,2:T(2,128)(2,1)S(1)} %divide_convert_fusion), kind=kOutput, calls=%fused_computation.13 | convolution fusion | flops 524288 | bytes 270336 | tf_op jit(solution)/shard_map/rihl,rlhd->rihd/dot_general | solution.py:45
  28.1 21.7 %all-gather.2.cloned.1.call-done = bf16[8192,64]{0,1:T(8,128)(2,1)} async-done(((bf16[512,64]{0,1:T(8,128)(2,1)}), bf16[8192,64]{0,1:T(8,128)(2,1)}) %all-gather.2.cloned.1.call-update) | async-done | bytes 1048592 | tf_op jit(solution)/shard_map/all_gather | solution.py:79
  49.8 2.7 %fusion.1 = bf16[128,8192]{1,0:T(8,128)(2,1)S(1)} fusion(bf16[8192,64]{0,1:T(8,128)(2,1)} %all-gather.2.cloned.1.call-done, bf16[128,8192]{1,0:T(8,128)(2,1)} %param.14, bf16[64,512]{1,0:T(8,128)(2,1)S(1)} %all_gather.6, s32[]{:T(128)S(6)} %select_n.17), kind=kOutput, calls=%fused_computation.2 | convolution fusion | flops 138412032 | bytes 5259268 | tf_op jit(solution)/shard_map/dot_general | solution.py:77
  52.4 0.0 copy-start.1
  52.5 0.0 copy-start.2
  52.5 0.0 copy-start.3
  52.5 1.4 %fusion.2 = f32[4,2,8192]{2,0,1:T(4,128)} fusion(bf16[128,8192]{1,0:T(8,128)(2,1)S(1)} %fusion.1, f32[4,2,128]{2,1,0:T(2,128)S(1)} %fusion.16, f32[4,2,128]{2,1,0:T(2,128)S(1)} %fusion.9), kind=kOutput, calls=%fused_computation.3 | convolution fusion | flops 16779264 | bytes 2367488 | tf_op jit(solution)/shard_map/dot_general | solution.py:87
  53.8 0.0 all-reduce.2.cloned.1.call-update
  53.9 35.0 %all-reduce.2.cloned.1.call-done = f32[4,2,8192]{2,0,1:T(4,128)} async-done(((f32[4,2,8192]{2,0,1:T(4,128)}), f32[4,2,8192]{2,0,1:T(4,128)}) %all-reduce.2.cloned.1.call-update) | async-done | bytes 262160 | tf_op jit(solution)/shard_map/psum | solution.py:91
  88.8 1.2 %multiply_reduce_fusion = f32[4,2]{0,1:T(2,128)S(1)} fusion(f32[4,2,8192]{2,0,1:T(4,128)} %all-reduce.2.cloned.1.call-done, bf16[4,2,8192]{2,1,0:T(2,128)(2,1)S(1)} %copy-done.2), kind=kLoop, calls=%fused_computation.16 | loop fusion | flops 262136 | bytes 393248 | tf_op jit(solution)/shard_map/reduce_sum | solution.py:93
  90.1 1.1 %multiply_convert_fusion = bf16[4,2,8192]{2,0,1:T(4,128)(2,1)S(1)} fusion(f32[4,2,8192]{2,0,1:T(4,128)} %all-reduce.2.cloned.1.call-done, f32[8192]{0:T(1024)S(1)} %copy-done.3, f32[4,2]{0,1:T(2,128)S(1)} %add_rsqrt_fusion, bf16[4,2,8192]{2,1,0:T(2,128)(2,1)S(1)} %copy-done.2), kind=kLoop, calls=%fused_computation.15 | loop fusion | flops 327680 | bytes 557088 | tf_op jit(solution)/shard_map/convert_element_type | solution.py:94
  91.2 0.8 copy.17
  92.0 0.0 copy-done.1
  (6 shorter events, 0.0 us)
Async XLA Ops:
  7.2 1.5 %copy-start = (bf16[4,2,128]{2,1,0:T(2,128)(2,1)S(1)}, bf16[4,2,128]{2,1,0:T(2,128)(2,1)}, u32[]{:S(2)}) copy-start(bf16[4,2,128]{2,1,0:T(2,128)(2,1)} %param.10) | copy-start | bytes 6148
  7.2 42.6 %all-gather.2.cloned.1.call-start = ((), (), s32[]{:S(2)}) async-start(), calls=%async_computation | async-start | bytes 1114112 | tf_op jit(solution)/shard_map/all_gather | solution.py:79
  7.9 80.9 %all-reduce.2.cloned.1.call-start = ((), (), s32[]{:S(2)}) async-start(), calls=%async_computation.1 | async-start | bytes 524288 | tf_op jit(solution)/shard_map/psum | solution.py:91
  52.4 39.5 %copy-start.1 = (bf16[128,8192]{1,0:T(8,128)(2,1)}, bf16[128,8192]{1,0:T(8,128)(2,1)S(1)}, u32[]{:S(2)}) copy-start(bf16[128,8192]{1,0:T(8,128)(2,1)S(1)} %fusion.1) | copy-start | bytes 6291460
  52.5 36.4 %copy-start.2 = (bf16[4,2,8192]{2,1,0:T(2,128)(2,1)S(1)}, bf16[4,2,8192]{2,1,0:T(2,128)(2,1)}, u32[]{:S(2)}) copy-start(bf16[4,2,8192]{2,1,0:T(2,128)(2,1)} %param.9) | copy-start | bytes 393220
  52.5 37.6 %copy-start.3 = (f32[8192]{0:T(1024)S(1)}, f32[8192]{0:T(1024)}, u32[]{:S(2)}) copy-start(f32[8192]{0:T(1024)} %param.17) | copy-start | bytes 98308
Sparse Core Ops, SparseCore 0:
  10.2 39.5 all-gather.1
  54.0 34.8 all-reduce.1
where the time goes:
time: 99.1 us; the launch traced here: 98.8 us
  waiting for transfers between devices  57.3 us (58%)
  blocking collectives  15.2 us (15%)
  between operations  14.1 us (14%)
  matrix products  7.99 us (8%)
  other arithmetic  3.35 us (3%)
    psum x1, waiting for transfers between devices, per_device(): summed = lax.psum(partial_value, 'tensor')  35 us
    all_gather x1, waiting for transfers between devices, per_device(): lax.all_gather(adapter_up_factor, ('tensor', 'replica'), axis=0, tiled=True)  21.7 us
    all_gather x1, blocking collectives, per_device(): lax.all_gather(adapter_down_factor, 'tensor', axis=0, tiled=True)  15.2 us
    dot_general x1, matrix products, per_device(): lax.dot_general(a_columns, lax.all_gather(adapter_up_factor, ('tensor', '...  2.65 us
  transfers between devices with their start and end apart: 2, of which 2 were waited for; matrix products, arithmetic and copies ran while one was open for 5% of the time, Pallas kernels for 0%

commit v1 on v0

--- a/solution.py
+++ b/solution.py
@@ -1,8 +1,11 @@
+import functools
 import math
 
 import jax
 import jax.numpy as jnp
 from jax import lax
+from jax.experimental import pallas as pl
+from jax.experimental.pallas import tpu as pltpu
 from jax.sharding import PartitionSpec as P
 
 HEAD_SIZE = 128
@@ -95,9 +98,430 @@
     return (normed, merged)
 
 
+MESH = pl.DeviceIdType.MESH
+F32 = jnp.float32
+BF16 = jnp.bfloat16
+
+
+def fused_kernel(
+    sizes,
+    lengths_ref,
+    hidden_hbm,
+    query_hbm,
+    fresh_hbm,
+    cache_hbm,
+    weight_hbm,
+    down_hbm,
+    up_hbm,
+    gain_hbm,
+    normed_ref,
+    merged_hbm,
+    hidden_ref,
+    query_ref,
+    fresh_ref,
+    cache_ref,
+    weight_ref,
+    gain_ref,
+    down_all,
+    up_all,
+    queries,
+    fresh_rows,
+    hidden_rows,
+    context_out,
+    context_in,
+    part_out,
+    part_in,
+    square_out,
+    square_in,
+    resid_out,
+    resid_in,
+    own_sum,
+    own_resid,
+    load_sem,
+    store_sem,
+    z_send,
+    z_recv,
+    x_send,
+    x_recv,
+    c_send,
+    c_recv,
+    a_send,
+    a_recv,
+    ctx_send,
+    ctx_recv,
+    rs_send,
+    rs_recv,
+    sq_send,
+    sq_recv,
+    ag_send,
+    ag_recv,
+):
+    rows, steps, span, width, owned, n = sizes
+    count = rows * steps
+    part = width // n
+    half = part // 2
+    chunk = up_hbm.shape[1]
+    rank_part = down_hbm.shape[0]
+    t = lax.axis_index("tensor")
+    r = lax.axis_index("replica")
+    across = lax.rem(r + 2, 4)
+    beside = r + 1 - 2 * lax.rem(r, 2)
+    me = t * 4 + r
+
+    def ahead(k):
+        return lax.rem(t + k, n)
+
+    def behind(k):
+        return lax.rem(t + n - k, n)
+
+    def remote(source, target, send, recv, device):
+        return pltpu.make_async_remote_copy(
+            src_ref=source,
+            dst_ref=target,
+            send_sem=send,
+            recv_sem=recv,
+            device_id=device,
+            device_id_type=MESH,
+        )
+
+    mine = pl.ds(pl.multiple_of(t * rank_part, rank_part), rank_part)
+    loads = [
+        pltpu.make_async_copy(a, b, load_sem.at[i])
+        for i, (a, b) in enumerate(
+            [
+                (up_hbm, up_all.at[me]),
+                (down_hbm, down_all.at[mine]),
+                (query_hbm, query_ref),
+                (fresh_hbm, fresh_ref),
+                (cache_hbm, cache_ref),
+                (weight_hbm, weight_ref),
+                (hidden_hbm, hidden_ref),
+                (gain_hbm, gain_ref),
+            ]
+        )
+    ]
+    for load in loads:
+        load.start()
+
+    barrier = pltpu.get_barrier_semaphore()
+    for k in range(1, n):
+        pl.semaphore_signal(barrier, inc=1, device_id={"tensor": ahead(k)}, device_id_type=MESH)
+    pl.semaphore_signal(barrier, inc=1, device_id={"replica": across}, device_id_type=MESH)
+    pl.semaphore_signal(barrier, inc=1, device_id={"replica": beside}, device_id_type=MESH)
+
+    z_copies = [
+        remote(up_all.at[me], up_all.at[me], z_send.at[k - 1], z_recv.at[k - 1], {"tensor": ahead(k)})
+        for k in range(1, n)
+    ]
+    x_copies = []
+    c_copies = []
+    for k in range(n):
+        near = behind(k) * 4 + r
+        far = behind(k) * 4 + across
+        x_copies.append(
+            remote(up_all.at[near], up_all.at[near], x_send.at[k], x_recv.at[k], {"replica": across})
+        )
+        for j, slot in enumerate((near, far)):
+            i = 2 * k + j
+            c_copies.append(
+                remote(up_all.at[slot], up_all.at[slot], c_send.at[i], c_recv.at[i], {"replica": beside})
+            )
+    a_copies = [
+        remote(
+            down_all.at[mine], down_all.at[mine], a_send.at[k - 1], a_recv.at[k - 1], {"tensor": ahead(k)}
+        )
+        for k in range(1, n)
+    ]
+
+    loads[0].wait()
+    loads[1].wait()
+    pl.semaphore_wait(barrier, n + 1)
+    x_copies[0].start()
+    c_copies[0].start()
+    for k in (2, 1, 3):
+        z_copies[k - 1].start()
+    for copy in a_copies:
+        copy.start()
+
+    loads[2].wait()
+    loads[3].wait()
+    for i in range(rows):
+        queries[i * steps : (i + 1) * steps, :] = query_ref[i].astype(F32)
+        fresh_rows[i * steps : (i + 1) * steps, :] = fresh_ref[i].astype(F32)
+    q = queries[...].astype(BF16)
+    fresh = fresh_rows[...].astype(BF16)
+    scale_factor = 1.0 / math.sqrt(HEAD_SIZE)
+    contract = (((1,), (1,)), ((), ()))
+    loads[4].wait()
+    keys = cache_ref[:, :, :HEAD_SIZE].reshape(rows * span, HEAD_SIZE)
+    values = cache_ref[:, :, HEAD_SIZE:].reshape(rows * span, HEAD_SIZE)
+    older = lax.dot_general(q, keys, contract, preferred_element_type=F32) * scale_factor
+    newer = lax.dot_general(
+        q, fresh[:, :HEAD_SIZE], contract, preferred_element_type=F32
+    ) * scale_factor
+    row = lax.broadcasted_iota(jnp.int32, (count, rows * span), 0)
+    column = lax.broadcasted_iota(jnp.int32, (count, rows * span), 1)
+    low = (row // steps) * span
+    high = low
+    for i in range(rows):
+        high = jnp.where(row // steps == i, i * span + lengths_ref[i], high)
+    older = jnp.where((column >= low) & (column < high), older, -1e30)
+    row = lax.broadcasted_iota(jnp.int32, (count, count), 0)
+    column = lax.broadcasted_iota(jnp.int32, (count, count), 1)
+    keep = (row // steps == column // steps) & (column <= row)
+    newer = jnp.where(keep, newer, -1e30)
+    top = jnp.maximum(
+        jnp.max(older, axis=1, keepdims=True), jnp.max(newer, axis=1, keepdims=True)
+    )
+    older = jnp.exp(older - top)
+    newer = jnp.exp(newer - top)
+    total = jnp.sum(older, axis=1, keepdims=True) + jnp.sum(newer, axis=1, keepdims=True)
+    older = (older / total).astype(BF16)
+    newer = (newer / total).astype(BF16)
+    context = jnp.dot(older, values, preferred_element_type=F32)
+    context = context + jnp.dot(newer, fresh[:, HEAD_SIZE:], preferred_element_type=F32)
+    context16 = jnp.concatenate([context, jnp.zeros_like(context)], axis=0).astype(BF16)
+    context_out[...] = context16
+    ctx_copies = [
+        remote(
+            context_out,
+            context_in.at[k - 1],
+            ctx_send.at[k - 1],
+            ctx_recv.at[k - 1],
+            {"tensor": ahead(k)},
+        )
+        for k in range(1, n)
+    ]
+    for copy in ctx_copies:
+        copy.start()
+
+    def columns(owner):
+        return pl.ds(pl.multiple_of(owner * part, part), part)
+
+    context = context_out[...]
+    loads[5].wait()
+    rs_copies = [None] * n
+    for k in (2, 1, 3):
+        product = jnp.dot(context, weight_ref[:, columns(ahead(k))], preferred_element_type=F32)
+        part_out[k - 1] = jnp.concatenate(
+            [product[:count, :half], product[:count, half:]], axis=0
+        ).astype(BF16)
+        rs_copies[k] = remote(
+            part_out.at[k - 1],
+            part_in.at[k - 1],
+            rs_send.at[k - 1],
+            rs_recv.at[k - 1],
+            {"tensor": ahead(k)},
+        )
+        rs_copies[k].start()
+    x_copies[0].wait_recv()
+    c_copies[1].start()
+    for k in range(1, n):
+        z_copies[k - 1].wait_recv()
+        x_copies[k].start()
+        c_copies[2 * k].start()
+    loads[6].wait()
+    for i in range(rows):
+        hidden_rows[i * steps : (i + 1) * steps, :] = hidden_ref[i, :, columns(t)].astype(F32)
+    product = jnp.dot(context, weight_ref[:, columns(t)], preferred_element_type=F32)
+    own_sum[...] = product[:count] + hidden_rows[...]
+
+    for copy in a_copies:
+        copy.wait_recv()
+    head = pl.ds(pl.multiple_of(t * owned, owned), owned)
+    own_down = (down_all[:, head].astype(F32) * ADAPTER_SCALE).T.astype(BF16)
+    stores = []
+
+    def merge(slot):
+        place = pl.ds(pl.multiple_of(slot * chunk, chunk), chunk)
+        update = jnp.dot(own_down, up_all[slot], preferred_element_type=F32)
+        weight_ref[:, place] = (weight_ref[:, place].astype(F32) + update).astype(BF16)
+        copy = pltpu.make_async_copy(
+            weight_ref.at[:, place], merged_hbm.at[:, place], store_sem.at[len(stores)]
+        )
+        copy.start()
+        stores.append(copy)
+
+    for k in range(n):
+        merge(behind(k) * 4 + r)
+
+    for copy in ctx_copies:
+        copy.wait_recv()
+    inner = jnp.dot(context, own_down, preferred_element_type=F32)
+    for k in range(1, n):
+        other = pl.ds(pl.multiple_of(behind(k) * owned, owned), owned)
+        inner = inner + ADAPTER_SCALE * lax.dot_general(
+            context_in[k - 1], down_all[:, other], contract, preferred_element_type=F32
+        )
+    inner = inner[:count]
+    upper = inner.astype(BF16).astype(F32)
+    inner = jnp.concatenate([upper, inner - upper], axis=0).astype(BF16)
+    c_copies[0].wait_recv()
+    c_copies[1].wait_recv()
+    for k in range(1, n):
+        rs_copies[k].wait_recv()
+    squares = jnp.zeros((count, 1), F32)
+    pieces = []
+    for j in range(4):
+        place = slice(j * chunk, (j + 1) * chunk)
+        term = jnp.dot(inner, up_all[t * 4 + j], preferred_element_type=F32)
+        value = own_sum[:, place] + term[:count] + term[count:]
+        for k in range(1, n):
+            top_rows = (j * chunk) // half * count
+            start = (j * chunk) % half
+            value = value + part_in[k - 1, :, start : start + chunk].astype(F32)[
+                top_rows : top_rows + count
+            ]
+        squares = squares + jnp.sum(value * value, axis=1, keepdims=True)
+        own_resid[:, place] = value
+        pieces.append(value)
+    square_out[...] = jnp.broadcast_to(squares, square_out.shape)
+    resid_out[...] = jnp.concatenate(
+        [
+            jnp.concatenate([pieces[0], pieces[1]], axis=1),
+            jnp.concatenate([pieces[2], pieces[3]], axis=1),
+        ],
+        axis=0,
+    ).astype(BF16)
+    ag_copies = []
+    for k in (2, 1, 3):
+        device = {"tensor": ahead(k)}
+        copies = [
+            remote(square_out, square_in.at[k - 1], sq_send.at[k - 1], sq_recv.at[k - 1], device),
+            remote(resid_out, resid_in.at[k - 1], ag_send.at[k - 1], ag_recv.at[k - 1], device),
+        ]
+        for copy in copies:
+            copy.start()
+        ag_copies.append((k, copies))
+
+    for k in range(1, n):
+        x_copies[k].wait_recv()
+        c_copies[2 * k + 1].start()
+    for k in range(n):
+        merge(behind(k) * 4 + across)
+    opposite = lax.rem(beside + 2, 4)
+    for k in range(n):
+        if k:
+            c_copies[2 * k].wait_recv()
+        merge(behind(k) * 4 + beside)
+    for k in range(n):
+        if k:
+            c_copies[2 * k + 1].wait_recv()
+        merge(behind(k) * 4 + opposite)
+
+    for k, copies in ag_copies:
+        copies[0].wait_recv()
+        squares = squares + square_in[k - 1, :, :1]
+    factor = lax.rsqrt(squares / width + EPS)
+    loads[7].wait()
+    value = own_resid[...] * factor * gain_ref[:, columns(t)]
+    for i in range(rows):
+        normed_ref[i, :, columns(t)] = value[i * steps : (i + 1) * steps].astype(BF16)
+    for k, copies in ag_copies:
+        copies[1].wait_recv()
+        arrived = resid_in[k - 1].astype(F32)
+        value = jnp.concatenate([arrived[:count], arrived[count:]], axis=1)
+        place = columns(behind(k))
+        value = value * factor * gain_ref[:, place]
+        for i in range(rows):
+            normed_ref[i, :, place] = value[i * steps : (i + 1) * steps].astype(BF16)
+
+    for copy in z_copies + x_copies + c_copies + a_copies + ctx_copies + rs_copies[1:]:
+        copy.wait_send()
+    for k, copies in ag_copies:
+        for copy in copies:
+            copy.wait_send()
+    for copy in stores:
+        copy.wait()
+
+
+def fused(
+    hidden,
+    query,
+    incoming_key_value,
+    cache,
+    lengths,
+    output_projection_weight,
+    adapter_down_factor,
+    adapter_up_factor,
+    gain,
+):
+    rows, steps, width = hidden.shape
+    span = cache.shape[1]
+    owned = output_projection_weight.shape[0]
+    n = adapter_down_factor.shape[1] // owned
+    rank = adapter_up_factor.shape[1]
+    chunk = adapter_up_factor.shape[0]
+    count = rows * steps
+    part = width // n
+    half = part // 2
+    both = 2 * HEAD_SIZE
+    anywhere = pl.BlockSpec(memory_space=pl.ANY)
+    dma = pltpu.SemaphoreType.DMA
+    peers = n - 1
+    return pl.pallas_call(
+        functools.partial(fused_kernel, (rows, steps, span, width, owned, n)),
+        out_shape=(
+            jax.ShapeDtypeStruct((rows, steps, width), BF16),
+            jax.ShapeDtypeStruct((owned, width), BF16),
+        ),
+        in_specs=[pl.BlockSpec(memory_space=pltpu.SMEM)] + [anywhere] * 8,
+        out_specs=(pl.BlockSpec(memory_space=pltpu.VMEM), anywhere),
+        scratch_shapes=[
+            pltpu.VMEM((rows, steps, width), BF16),
+            pltpu.VMEM((rows, steps, HEAD_SIZE), BF16),
+            pltpu.VMEM((rows, steps, both), BF16),
+            pltpu.VMEM((rows, span, both), BF16),
+            pltpu.VMEM((owned, width), BF16),
+            pltpu.VMEM((1, width), F32),
+            pltpu.VMEM((rank, n * owned), BF16),
+            pltpu.VMEM((4 * n, rank, chunk), BF16),
+            pltpu.VMEM((count, HEAD_SIZE), F32),
+            pltpu.VMEM((count, both), F32),
+            pltpu.VMEM((count, part), F32),
+            pltpu.VMEM((2 * count, HEAD_SIZE), BF16),
+            pltpu.VMEM((peers, 2 * count, HEAD_SIZE), BF16),
+            pltpu.VMEM((peers, 2 * count, half), BF16),
+            pltpu.VMEM((peers, 2 * count, half), BF16),
+            pltpu.VMEM((count, 128), F32),
+            pltpu.VMEM((peers, count, 128), F32),
+            pltpu.VMEM((2 * count, half), BF16),
+            pltpu.VMEM((peers, 2 * count, half), BF16),
+            pltpu.VMEM((count, part), F32),
+            pltpu.VMEM((count, part), F32),
+            dma((8,)),
+            dma((4 * n,)),
+            dma((peers,)),
+            dma((peers,)),
+            dma((n,)),
+            dma((n,)),
+            dma((2 * n,)),
+            dma((2 * n,)),
+        ]
+        + [dma((peers,))] * 10,
+        compiler_params=pltpu.CompilerParams(
+            collective_id=0, has_side_effects=True, vmem_limit_bytes=24 * 2**20
+        ),
+        cost_estimate=pl.CostEstimate(
+            flops=2 * owned * width * (rank + count), bytes_accessed=6 * 2**20, transcendentals=0
+        ),
+    )(
+        lengths,
+        hidden,
+        query,
+        incoming_key_value.reshape(rows, steps, both),
+        cache.reshape(rows, span, both),
+        output_projection_weight,
+        adapter_down_factor,
+        adapter_up_factor.T,
+        gain.reshape(1, width),
+    )
+
+
 def solution(mesh):
+    fits = mesh.shape["tensor"] == 4 and mesh.shape["replica"] == 4
     return jax.shard_map(
-        per_device,
+        fused if fits else per_device,
         mesh=mesh,
         in_specs=(
             P(("groups", "replica"), None, None),

time: 99.1 us -> 34.2 us (0.35)
  waiting for transfers between devices: 57.3 us -> 0 us
  Pallas kernels: 0 us -> 23.2 us
  blocking collectives: 15.2 us -> 0 us
  between operations: 14.1 us -> 0.66 us
  local copies, waits for them, and re-layouts: 0.82 us -> 9.84 us
  matrix products: 7.99 us -> 0 us
  other arithmetic: 3.35 us -> 0 us
    psum x1 -> x0, waiting for transfers between devices: 35 us -> none  [per_device(): summed = lax.psum(partial_value, 'tensor')]
    pallas_call x0 -> x1, Pallas kernels: none -> 23.2 us  [fused(): pl.pallas_call(functools.partial(fused_kernel, (rows, steps, span, width,...]
    all_gather x1 -> x0, waiting for transfers between devices: 21.7 us -> none  [per_device(): lax.all_gather(adapter_up_factor, ('tensor', 'replica'), axis=0, tiled=True)]
    all_gather x1 -> x0, blocking collectives: 15.2 us -> none  [per_device(): lax.all_gather(adapter_down_factor, 'tensor', axis=0, tiled=True)]
    unnamed x9 -> x20, local copies, waits for them, and re-layouts: 0.82 us -> 9.84 us
    dot_general x6 -> x0, matrix products: 7.99 us -> none  [the longest x1 2.65 us: per_device(): lax.dot_general(a_columns, lax.all_gather(adapter_up_factor, ('tensor', '...]
    reduce_sum x2 -> x0, other arithmetic: 1.39 us -> none  [the longest x1 1.22 us: per_device(): mean_square = jnp.mean(resid * resid, axis=-1, keepdims=True)]
    convert_element_type x2 -> x0, other arithmetic: 1.21 us -> none  [the longest x1 1.12 us: per_device(): normed = (resid * lax.rsqrt(mean_square + EPS) * gain).astype(jnp.bfloat16)]
  transfers between devices with their start and end apart: 2 -> 0, of which waited for: 2 -> 0; matrix products, arithmetic and copies ran while one was open for 5% -> 0% of each run, Pallas kernels for 0% -> 0%
where the time goes in v1:
time: 34.2 us; the launch traced here: 33.7 us
  Pallas kernels  23.2 us (68%)
  local copies, waits for them, and re-layouts  9.84 us (29%)
  between operations  0.66 us (2%)
    pallas_call x1, Pallas kernels, fused(): pl.pallas_call(functools.partial(fused_kernel, (rows, steps, span, width,...  23.2 us
    unnamed x20, local copies, waits for them, and re-layouts  9.84 us

profile of v1, /device:TPU:0, one launch (start us, length us, event | category | flops | bytes accessed | tf_op | source)
XLA Modules:
  0.0 33.7 jit_solution(9735738520842559338)
XLA Ops:
  0.6 0.0 copy-start
  0.6 1.6 %copy-done = bf16[128,8192]{1,0:T(8,128)(2,1)S(1)} copy-done((bf16[128,8192]{1,0:T(8,128)(2,1)S(1)}, bf16[128,8192]{1,0:T(8,128)(2,1)}, u32[]{:S(2)}) %copy-start) | copy-done | bytes 2097176
  2.2 0.0 copy-start.1
  2.2 1.0 %copy-done.1 = bf16[4,256,1,256]{3,1,2,0:T(8,128)(2,1)S(1)} copy-done((bf16[4,256,1,256]{3,1,2,0:T(8,128)(2,1)S(1)}, bf16[4,256,1,256]{3,1,2,0:T(8,128)(2,1)}, u32[]{:S(2)}) %copy-start.1) | copy-done | bytes 524312
  3.3 0.0 copy-start.2
  3.3 0.9 %copy-done.2 = bf16[4,2,8192]{2,1,0:T(2,128)(2,1)S(1)} copy-done((bf16[4,2,8192]{2,1,0:T(2,128)(2,1)S(1)}, bf16[4,2,8192]{2,1,0:T(2,128)(2,1)}, u32[]{:S(2)}) %copy-start.2) | copy-done | bytes 131096
  4.2 0.0 copy-start.3
  4.2 0.8 %copy-done.3 = bf16[512,64]{0,1:T(8,128)(2,1)S(1)} copy-done((bf16[512,64]{0,1:T(8,128)(2,1)S(1)}, bf16[512,64]{0,1:T(8,128)(2,1)}, u32[]{:S(2)}) %copy-start.3) | copy-done | bytes 65560
  5.0 0.0 copy-start.4
  5.0 0.8 %copy-done.4 = f32[8192]{0:T(1024)S(1)} copy-done((f32[8192]{0:T(1024)S(1)}, f32[8192]{0:T(1024)}, u32[]{:S(2)}) %copy-start.4) | copy-done | bytes 32792
  5.8 0.0 copy-start.5
  5.8 0.7 %copy-done.5 = bf16[16,512]{1,0:T(8,128)(2,1)S(1)} copy-done((bf16[16,512]{1,0:T(8,128)(2,1)S(1)}, bf16[16,512]{1,0:T(8,128)(2,1)}, u32[]{:S(2)}) %copy-start.5) | copy-done | bytes 16408
  6.5 0.0 copy-start.6
  6.5 0.7 %copy-done.6 = bf16[4,2,1,256]{3,1,2,0:T(2,128)(2,1)S(1)} copy-done((bf16[4,2,1,256]{3,1,2,0:T(2,128)(2,1)S(1)}, bf16[4,2,1,256]{3,1,2,0:T(2,128)(2,1)}, u32[]{:S(2)}) %copy-start.6) | copy-done | bytes 4120
  7.2 0.0 copy-start.7
  7.2 0.7 %copy-done.7 = bf16[4,2,128]{2,1,0:T(2,128)(2,1)S(1)} copy-done((bf16[4,2,128]{2,1,0:T(2,128)(2,1)S(1)}, bf16[4,2,128]{2,1,0:T(2,128)(2,1)}, u32[]{:S(2)}) %copy-start.7) | copy-done | bytes 2072
  7.9 0.0 copy-start.8
  7.9 0.7 %copy-done.8 = s32[4]{0:T(128)S(1)} copy-done((s32[4]{0:T(128)S(1)}, s32[4]{0:T(128)}, u32[]{:S(2)}) %copy-start.8) | copy-done | bytes 40
  8.5 23.2 %shard_map.104 = (bf16[4,2,8192]{2,1,0:T(2,128)(2,1)S(1)}, bf16[128,8192]{1,0:T(8,128)(2,1)S(1)}) custom-call(s32[4]{0:T(128)S(1)} %copy-done.8, bf16[4,2,8192]{2,1,0:T(2,128)(2,1)S(1)} %copy-done.2, bf16[4,2,128]{2,1,0:T(2,128)(2,1)S(1)} %copy-done.7, bf16[4,2,256]{2,1,0:T(2,128)(2,1)S(1)} %bitcast.7, bf16[4,256,256]{2,1,0:T(8,128)(2,1)S(1)} %bitcast.4, ...), custom_call_target="tpu_custom_call" | custom-call | flops 150994944 | bytes 6291456 | tf_op jit(solution)/shard_map/pallas_call | solution.py:462
  31.8 0.7 %copy.13 = bf16[4,2,8192]{2,1,0:T(2,128)(2,1)} copy(bf16[4,2,8192]{2,1,0:T(2,128)(2,1)S(1)} %get-tuple-element.4) | data formatting | bytes 262144
  32.4 1.3 %copy.14 = bf16[128,8192]{1,0:T(8,128)(2,1)} copy(bf16[128,8192]{1,0:T(8,128)(2,1)S(1)} %get-tuple-element.5) | data formatting | bytes 4194304
Async XLA Ops:
  0.6 1.6 %copy-start = (bf16[128,8192]{1,0:T(8,128)(2,1)S(1)}, bf16[128,8192]{1,0:T(8,128)(2,1)}, u32[]{:S(2)}) copy-start(bf16[128,8192]{1,0:T(8,128)(2,1)} %weight_hbm.1) | copy-start | bytes 6291460
  2.2 1.0 %copy-start.1 = (bf16[4,256,1,256]{3,1,2,0:T(8,128)(2,1)S(1)}, bf16[4,256,1,256]{3,1,2,0:T(8,128)(2,1)}, u32[]{:S(2)}) copy-start(bf16[4,256,1,256]{3,1,2,0:T(8,128)(2,1)} %param.12) | copy-start | bytes 1572868
  3.3 0.9 %copy-start.2 = (bf16[4,2,8192]{2,1,0:T(2,128)(2,1)S(1)}, bf16[4,2,8192]{2,1,0:T(2,128)(2,1)}, u32[]{:S(2)}) copy-start(bf16[4,2,8192]{2,1,0:T(2,128)(2,1)} %hidden_hbm.1) | copy-start | bytes 393220
  4.2 0.8 %copy-start.3 = (bf16[512,64]{0,1:T(8,128)(2,1)S(1)}, bf16[512,64]{0,1:T(8,128)(2,1)}, u32[]{:S(2)}) copy-start(bf16[512,64]{0,1:T(8,128)(2,1)} %param.16) | copy-start | bytes 196612
  5.0 0.8 %copy-start.4 = (f32[8192]{0:T(1024)S(1)}, f32[8192]{0:T(1024)}, u32[]{:S(2)}) copy-start(f32[8192]{0:T(1024)} %param.17) | copy-start | bytes 98308
  5.8 0.7 %copy-start.5 = (bf16[16,512]{1,0:T(8,128)(2,1)S(1)}, bf16[16,512]{1,0:T(8,128)(2,1)}, u32[]{:S(2)}) copy-start(bf16[16,512]{1,0:T(8,128)(2,1)} %down_hbm.1) | copy-start | bytes 49156
  6.5 0.7 %copy-start.6 = (bf16[4,2,1,256]{3,1,2,0:T(2,128)(2,1)S(1)}, bf16[4,2,1,256]{3,1,2,0:T(2,128)(2,1)}, u32[]{:S(2)}) copy-start(bf16[4,2,1,256]{3,1,2,0:T(2,128)(2,1)} %param.11) | copy-start | bytes 12292
  7.2 0.7 %copy-start.7 = (bf16[4,2,128]{2,1,0:T(2,128)(2,1)S(1)}, bf16[4,2,128]{2,1,0:T(2,128)(2,1)}, u32[]{:S(2)}) copy-start(bf16[4,2,128]{2,1,0:T(2,128)(2,1)} %query_hbm.1) | copy-start | bytes 6148
  7.9 0.7 %copy-start.8 = (s32[4]{0:T(128)S(1)}, s32[4]{0:T(128)}, u32[]{:S(2)}) copy-start(s32[4]{0:T(128)} %lengths_ref.1) | copy-start | bytes 52

commit v2 on v1

--- a/solution.py
+++ b/solution.py
@@ -105,7 +105,7 @@
 
 def fused_kernel(
     sizes,
-    lengths_ref,
+    lengths_hbm,
     hidden_hbm,
     query_hbm,
     fresh_hbm,
@@ -115,7 +115,8 @@
     up_hbm,
     gain_hbm,
     normed_ref,
-    merged_hbm,
+    merged_ref,
+    lengths_ref,
     hidden_ref,
     query_ref,
     fresh_ref,
@@ -138,7 +139,6 @@
     own_sum,
     own_resid,
     load_sem,
-    store_sem,
     z_send,
     z_recv,
     x_send,
@@ -197,6 +197,7 @@
                 (weight_hbm, weight_ref),
                 (hidden_hbm, hidden_ref),
                 (gain_hbm, gain_ref),
+                (lengths_hbm, lengths_ref),
             ]
         )
     ]
@@ -253,6 +254,7 @@
     scale_factor = 1.0 / math.sqrt(HEAD_SIZE)
     contract = (((1,), (1,)), ((), ()))
     loads[4].wait()
+    loads[8].wait()
     keys = cache_ref[:, :, :HEAD_SIZE].reshape(rows * span, HEAD_SIZE)
     values = cache_ref[:, :, HEAD_SIZE:].reshape(rows * span, HEAD_SIZE)
     older = lax.dot_general(q, keys, contract, preferred_element_type=F32) * scale_factor
@@ -330,17 +332,11 @@
         copy.wait_recv()
     head = pl.ds(pl.multiple_of(t * owned, owned), owned)
     own_down = (down_all[:, head].astype(F32) * ADAPTER_SCALE).T.astype(BF16)
-    stores = []
 
     def merge(slot):
         place = pl.ds(pl.multiple_of(slot * chunk, chunk), chunk)
         update = jnp.dot(own_down, up_all[slot], preferred_element_type=F32)
-        weight_ref[:, place] = (weight_ref[:, place].astype(F32) + update).astype(BF16)
-        copy = pltpu.make_async_copy(
-            weight_ref.at[:, place], merged_hbm.at[:, place], store_sem.at[len(stores)]
-        )
-        copy.start()
-        stores.append(copy)
+        merged_ref[:, place] = (weight_ref[:, place].astype(F32) + update).astype(BF16)
 
     for k in range(n):
         merge(behind(k) * 4 + r)
@@ -431,7 +427,20 @@
     for k, copies in ag_copies:
         for copy in copies:
             copy.wait_send()
-    for copy in stores:
+
+
+def store_kernel(normed_ref, merged_ref, normed_hbm, merged_hbm, sem):
+    step = merged_ref.shape[0] // 8
+    copies = [
+        pltpu.make_async_copy(
+            merged_ref.at[i * step : (i + 1) * step], merged_hbm.at[i * step : (i + 1) * step], sem.at[i]
+        )
+        for i in range(8)
+    ]
+    copies.append(pltpu.make_async_copy(normed_ref, normed_hbm, sem.at[8]))
+    for copy in copies:
+        copy.start()
+    for copy in copies:
         copy.wait()
 
 
@@ -456,18 +465,20 @@
     part = width // n
     half = part // 2
     both = 2 * HEAD_SIZE
-    anywhere = pl.BlockSpec(memory_space=pl.ANY)
+    outside = pl.BlockSpec(memory_space=pltpu.HBM)
+    inside = pl.BlockSpec(memory_space=pltpu.VMEM)
     dma = pltpu.SemaphoreType.DMA
     peers = n - 1
-    return pl.pallas_call(
+    normed, merged = pl.pallas_call(
         functools.partial(fused_kernel, (rows, steps, span, width, owned, n)),
         out_shape=(
             jax.ShapeDtypeStruct((rows, steps, width), BF16),
             jax.ShapeDtypeStruct((owned, width), BF16),
         ),
-        in_specs=[pl.BlockSpec(memory_space=pltpu.SMEM)] + [anywhere] * 8,
-        out_specs=(pl.BlockSpec(memory_space=pltpu.VMEM), anywhere),
+        in_specs=[outside] * 9,
+        out_specs=(inside, inside),
         scratch_shapes=[
+            pltpu.SMEM((rows,), jnp.int32),
             pltpu.VMEM((rows, steps, width), BF16),
             pltpu.VMEM((rows, steps, HEAD_SIZE), BF16),
             pltpu.VMEM((rows, steps, both), BF16),
@@ -489,8 +500,7 @@
             pltpu.VMEM((peers, 2 * count, half), BF16),
             pltpu.VMEM((count, part), F32),
             pltpu.VMEM((count, part), F32),
-            dma((8,)),
-            dma((4 * n,)),
+            dma((9,)),
             dma((peers,)),
             dma((peers,)),
             dma((n,)),
@@ -500,22 +510,38 @@
         ]
         + [dma((peers,))] * 10,
         compiler_params=pltpu.CompilerParams(
-            collective_id=0, has_side_effects=True, vmem_limit_bytes=24 * 2**20
+            collective_id=0, has_side_effects=True, vmem_limit_bytes=16 * 2**20
         ),
         cost_estimate=pl.CostEstimate(
             flops=2 * owned * width * (rank + count), bytes_accessed=6 * 2**20, transcendentals=0
         ),
     )(
-        lengths,
-        hidden,
-        query,
-        incoming_key_value.reshape(rows, steps, both),
-        cache.reshape(rows, span, both),
-        output_projection_weight,
-        adapter_down_factor,
-        adapter_up_factor.T,
-        gain.reshape(1, width),
-    )
+        *[
+            pltpu.with_memory_space_constraint(operand, pltpu.HBM)
+            for operand in (
+                lengths,
+                hidden,
+                query,
+                incoming_key_value.reshape(rows, steps, both),
+                cache.reshape(rows, span, both),
+                output_projection_weight,
+                adapter_down_factor,
+                adapter_up_factor.T,
+                gain.reshape(1, width),
+            )
+        ]
+    )
+    return pl.pallas_call(
+        store_kernel,
+        out_shape=(
+            jax.ShapeDtypeStruct(normed.shape, BF16),
+            jax.ShapeDtypeStruct(merged.shape, BF16),
+        ),
+        in_specs=[inside, inside],
+        out_specs=(outside, outside),
+        scratch_shapes=[dma((9,))],
+        compiler_params=pltpu.CompilerParams(vmem_limit_bytes=16 * 2**20),
+    )(normed, merged)
 
 
 def solution(mesh):

time: 34.2 us -> 23.9 us (0.70)
  local copies, waits for them, and re-layouts: 9.84 us -> 0 us
    unnamed x20 -> x0, local copies, waits for them, and re-layouts: 9.84 us -> none
    pallas_call x1, Pallas kernels: 23.2 us -> 21.7 us  [fused(): pl.pallas_call(functools.partial(fused_kernel, (rows, steps, span, width,...]
    pallas_call x0 -> x1, Pallas kernels: none -> 1.42 us  [fused(): pl.pallas_call(store_kernel, out_shape=(jax.ShapeDtypeStruct(normed.shape...]
where the time goes in v2:
time: 23.9 us; the launch traced here: 23.8 us
  Pallas kernels  23.1 us (97%)
  between operations  0.64 us (3%)
    pallas_call x1, Pallas kernels, fused(): pl.pallas_call(functools.partial(fused_kernel, (rows, steps, span, width,...  21.7 us
    pallas_call x1, Pallas kernels, fused(): pl.pallas_call(store_kernel, out_shape=(jax.ShapeDtypeStruct(normed.shape...  1.42 us

profile of v2, /device:TPU:0, one launch (start us, length us, event | category | flops | bytes accessed | tf_op | source)
XLA Modules:
  0.0 23.8 jit_solution(11476947616041903551)
XLA Ops:
  0.6 21.7 %shard_map.104 = (bf16[4,2,8192]{2,1,0:T(2,128)(2,1)S(1)}, bf16[128,8192]{1,0:T(8,128)(2,1)S(1)}) custom-call(s32[4]{0:T(128)} %lengths_hbm.1, bf16[4,2,8192]{2,1,0:T(2,128)(2,1)} %hidden_hbm.1, bf16[4,2,128]{2,1,0:T(2,128)(2,1)} %query_hbm.1, bf16[4,2,256]{2,1,0:T(2,128)(2,1)} %bitcast.7, bf16[4,256,256]{2,1,0:T(8,128)(2,1)} %bitcast.4, ...), custom_call_target="tpu_custom_call" | custom-call | flops 150994944 | bytes 6291456 | tf_op jit(solution)/shard_map/pallas_call | solution.py:472
  22.4 1.4 %shard_map.105 = (bf16[4,2,8192]{2,1,0:T(2,128)(2,1)}, bf16[128,8192]{1,0:T(8,128)(2,1)}) custom-call(bf16[4,2,8192]{2,1,0:T(2,128)(2,1)S(1)} %get-tuple-element.4.normed_ref, bf16[128,8192]{1,0:T(8,128)(2,1)S(1)} %get-tuple-element.5.merged_ref), custom_call_target="tpu_custom_call" | custom-call | tf_op jit(solution)/shard_map/pallas_call | solution.py:534

commit v3 on v2

--- a/solution.py
+++ b/solution.py
@@ -101,6 +101,7 @@
 MESH = pl.DeviceIdType.MESH
 F32 = jnp.float32
 BF16 = jnp.bfloat16
+PIECES = 2
 
 
 def fused_kernel(
@@ -184,6 +185,18 @@
             device_id_type=MESH,
         )
 
+    def gather(source, slot, send, recv, device):
+        depth = up_hbm.shape[0] // PIECES
+        copies = []
+        for p in range(PIECES):
+            piece = slice(p * depth, (p + 1) * depth)
+            copies.append(
+                remote(
+                    source.at[piece], up_all.at[slot, piece], send.at[p], recv.at[p], device
+                )
+            )
+        return copies
+
     mine = pl.ds(pl.multiple_of(t * rank_part, rank_part), rank_part)
     loads = [
         pltpu.make_async_copy(a, b, load_sem.at[i])
@@ -210,22 +223,35 @@
     pl.semaphore_signal(barrier, inc=1, device_id={"replica": across}, device_id_type=MESH)
     pl.semaphore_signal(barrier, inc=1, device_id={"replica": beside}, device_id_type=MESH)
 
+    side = t // 2
+    inside = (t == 1) | (t == 2)
+    mate = t + 1 - 2 * lax.rem(t, 2)
+    sources = [t, mate, 2 - side, 3 - 3 * side]
+    nears = [source * 4 + r for source in sources]
+    fars = [source * 4 + across for source in sources]
+    landing = 1 + lax.rem(t + side + 1, 2)
     z_copies = [
-        remote(up_all.at[me], up_all.at[me], z_send.at[k - 1], z_recv.at[k - 1], {"tensor": ahead(k)})
-        for k in range(1, n)
+        gather(up_all.at[me], me, z_send.at[0], z_recv.at[0], {"tensor": mate}),
+        gather(up_all.at[me], me, z_send.at[1], z_recv.at[landing], {"tensor": 2 - side}),
+    ]
+    passed = [
+        gather(up_all.at[nears[k]], nears[k], z_send.at[k], z_recv.at[k - 1], {"tensor": mate})
+        for k in (2, 3)
+    ]
+    z_arrivals = [
+        gather(up_all.at[nears[k]], nears[k], z_send.at[0], z_recv.at[k - 1], {"tensor": mate})
+        for k in (1, 2, 3)
     ]
     x_copies = []
     c_copies = []
     for k in range(n):
-        near = behind(k) * 4 + r
-        far = behind(k) * 4 + across
         x_copies.append(
-            remote(up_all.at[near], up_all.at[near], x_send.at[k], x_recv.at[k], {"replica": across})
-        )
-        for j, slot in enumerate((near, far)):
+            gather(up_all.at[nears[k]], nears[k], x_send.at[k], x_recv.at[k], {"replica": across})
+        )
+        for j, slot in enumerate((nears[k], fars[k])):
             i = 2 * k + j
             c_copies.append(
-                remote(up_all.at[slot], up_all.at[slot], c_send.at[i], c_recv.at[i], {"replica": beside})
+                gather(up_all.at[slot], slot, c_send.at[i], c_recv.at[i], {"replica": beside})
             )
     a_copies = [
         remote(
@@ -237,10 +263,11 @@
     loads[0].wait()
     loads[1].wait()
     pl.semaphore_wait(barrier, n + 1)
-    x_copies[0].start()
-    c_copies[0].start()
-    for k in (2, 1, 3):
-        z_copies[k - 1].start()
+    for p in range(PIECES):
+        for copies in z_copies:
+            copies[p].start()
+        x_copies[0][p].start()
+        c_copies[0][p].start()
     for copy in a_copies:
         copy.start()
 
@@ -302,26 +329,37 @@
 
     context = context_out[...]
     loads[5].wait()
-    rs_copies = [None] * n
-    for k in (2, 1, 3):
-        product = jnp.dot(context, weight_ref[:, columns(ahead(k))], preferred_element_type=F32)
-        part_out[k - 1] = jnp.concatenate(
-            [product[:count, :half], product[:count, half:]], axis=0
-        ).astype(BF16)
-        rs_copies[k] = remote(
-            part_out.at[k - 1],
-            part_in.at[k - 1],
-            rs_send.at[k - 1],
-            rs_recv.at[k - 1],
-            {"tensor": ahead(k)},
-        )
-        rs_copies[k].start()
-    x_copies[0].wait_recv()
-    c_copies[1].start()
-    for k in range(1, n):
-        z_copies[k - 1].wait_recv()
-        x_copies[k].start()
-        c_copies[2 * k].start()
+    rs_copies = {}
+    for h in range(2):
+        for k in (2, 1, 3):
+            place = pl.ds(pl.multiple_of(ahead(k) * part + h * half, half), half)
+            product = jnp.dot(context, weight_ref[:, place], preferred_element_type=F32)
+            i = 2 * (k - 1) + h
+            part_out[i] = jnp.concatenate(
+                [product[:count, :chunk], product[:count, chunk:]], axis=0
+            ).astype(BF16)
+            rs_copies[h, k] = remote(
+                part_out.at[i], part_in.at[i], rs_send.at[i], rs_recv.at[i], {"tensor": ahead(k)}
+            )
+            rs_copies[h, k].start()
+    for p in range(PIECES):
+        x_copies[0][p].wait_recv()
+        c_copies[1][p].start()
+    for p in range(PIECES):
+        z_arrivals[0][p].wait_recv()
+        x_copies[1][p].start()
+        c_copies[2][p].start()
+
+    def spread(forward):
+        for k in (2, 3):
+            for p in range(PIECES):
+                z_arrivals[k - 1][p].wait_recv()
+                if forward:
+                    passed[k - 2][p].start()
+                x_copies[k][p].start()
+                c_copies[2 * k][p].start()
+
+    pl.when(inside)(lambda: spread(True))
     loads[6].wait()
     for i in range(rows):
         hidden_rows[i * steps : (i + 1) * steps, :] = hidden_ref[i, :, columns(t)].astype(F32)
@@ -337,9 +375,6 @@
         place = pl.ds(pl.multiple_of(slot * chunk, chunk), chunk)
         update = jnp.dot(own_down, up_all[slot], preferred_element_type=F32)
         merged_ref[:, place] = (weight_ref[:, place].astype(F32) + update).astype(BF16)
-
-    for k in range(n):
-        merge(behind(k) * 4 + r)
 
     for copy in ctx_copies:
         copy.wait_recv()
@@ -352,81 +387,95 @@
     inner = inner[:count]
     upper = inner.astype(BF16).astype(F32)
     inner = jnp.concatenate([upper, inner - upper], axis=0).astype(BF16)
-    c_copies[0].wait_recv()
-    c_copies[1].wait_recv()
-    for k in range(1, n):
-        rs_copies[k].wait_recv()
+    for copy in c_copies[0] + c_copies[1]:
+        copy.wait_recv()
     squares = jnp.zeros((count, 1), F32)
-    pieces = []
-    for j in range(4):
-        place = slice(j * chunk, (j + 1) * chunk)
-        term = jnp.dot(inner, up_all[t * 4 + j], preferred_element_type=F32)
-        value = own_sum[:, place] + term[:count] + term[count:]
+    ag_copies = []
+    sq_copies = []
+    for h in range(2):
         for k in range(1, n):
-            top_rows = (j * chunk) // half * count
-            start = (j * chunk) % half
-            value = value + part_in[k - 1, :, start : start + chunk].astype(F32)[
-                top_rows : top_rows + count
-            ]
-        squares = squares + jnp.sum(value * value, axis=1, keepdims=True)
-        own_resid[:, place] = value
-        pieces.append(value)
-    square_out[...] = jnp.broadcast_to(squares, square_out.shape)
-    resid_out[...] = jnp.concatenate(
-        [
-            jnp.concatenate([pieces[0], pieces[1]], axis=1),
-            jnp.concatenate([pieces[2], pieces[3]], axis=1),
-        ],
-        axis=0,
-    ).astype(BF16)
-    ag_copies = []
-    for k in (2, 1, 3):
-        device = {"tensor": ahead(k)}
-        copies = [
-            remote(square_out, square_in.at[k - 1], sq_send.at[k - 1], sq_recv.at[k - 1], device),
-            remote(resid_out, resid_in.at[k - 1], ag_send.at[k - 1], ag_recv.at[k - 1], device),
-        ]
-        for copy in copies:
+            rs_copies[h, k].wait_recv()
+        pieces = []
+        for j in range(2):
+            place = slice((2 * h + j) * chunk, (2 * h + j + 1) * chunk)
+            term = jnp.dot(inner, up_all[t * 4 + 2 * h + j], preferred_element_type=F32)
+            value = own_sum[:, place] + term[:count] + term[count:]
+            for k in range(1, n):
+                value = value + part_in[2 * (k - 1) + h].astype(F32)[j * count : (j + 1) * count]
+            squares = squares + jnp.sum(value * value, axis=1, keepdims=True)
+            own_resid[:, place] = value
+            pieces.append(value)
+        resid_out[h] = jnp.concatenate(pieces, axis=0).astype(BF16)
+        if h:
+            square_out[...] = jnp.broadcast_to(squares, square_out.shape)
+        for k in (2, 1, 3):
+            device = {"tensor": ahead(k)}
+            i = 2 * (k - 1) + h
+            if h:
+                copy = remote(
+                    square_out, square_in.at[k - 1], sq_send.at[k - 1], sq_recv.at[k - 1], device
+                )
+                copy.start()
+                sq_copies.append(copy)
+            copy = remote(resid_out.at[h], resid_in.at[i], ag_send.at[i], ag_recv.at[i], device)
             copy.start()
-        ag_copies.append((k, copies))
-
-    for k in range(1, n):
-        x_copies[k].wait_recv()
-        c_copies[2 * k + 1].start()
+            ag_copies.append((h, k, copy))
+        if not h:
+            for p in range(PIECES):
+                x_copies[1][p].wait_recv()
+                c_copies[3][p].start()
+
+    pl.when(jnp.logical_not(inside))(lambda: spread(False))
     for k in range(n):
-        merge(behind(k) * 4 + across)
+        merge(nears[k])
+
+    for k in range(2, n):
+        for p in range(PIECES):
+            x_copies[k][p].wait_recv()
+            c_copies[2 * k + 1][p].start()
+    for k in range(n):
+        merge(fars[k])
     opposite = lax.rem(beside + 2, 4)
     for k in range(n):
         if k:
-            c_copies[2 * k].wait_recv()
-        merge(behind(k) * 4 + beside)
+            for copy in c_copies[2 * k]:
+                copy.wait_recv()
+        merge(sources[k] * 4 + beside)
     for k in range(n):
         if k:
-            c_copies[2 * k + 1].wait_recv()
-        merge(behind(k) * 4 + opposite)
-
-    for k, copies in ag_copies:
-        copies[0].wait_recv()
+            for copy in c_copies[2 * k + 1]:
+                copy.wait_recv()
+        merge(sources[k] * 4 + opposite)
+
+    for copy in sq_copies:
+        copy.wait_recv()
+    for k in range(1, n):
         squares = squares + square_in[k - 1, :, :1]
     factor = lax.rsqrt(squares / width + EPS)
     loads[7].wait()
     value = own_resid[...] * factor * gain_ref[:, columns(t)]
     for i in range(rows):
         normed_ref[i, :, columns(t)] = value[i * steps : (i + 1) * steps].astype(BF16)
-    for k, copies in ag_copies:
-        copies[1].wait_recv()
-        arrived = resid_in[k - 1].astype(F32)
+    for h, k, copy in ag_copies:
+        copy.wait_recv()
+        arrived = resid_in[2 * (k - 1) + h].astype(F32)
         value = jnp.concatenate([arrived[:count], arrived[count:]], axis=1)
-        place = columns(behind(k))
+        place = pl.ds(pl.multiple_of(behind(k) * part + h * half, half), half)
         value = value * factor * gain_ref[:, place]
         for i in range(rows):
             normed_ref[i, :, place] = value[i * steps : (i + 1) * steps].astype(BF16)
 
-    for copy in z_copies + x_copies + c_copies + a_copies + ctx_copies + rs_copies[1:]:
-        copy.wait_send()
-    for k, copies in ag_copies:
+    for copy in passed[0] + passed[1]:
+        pl.when(inside)(copy.wait_send)
+    for copies in z_copies + x_copies + c_copies:
         for copy in copies:
             copy.wait_send()
+    for copy in a_copies + ctx_copies + sq_copies:
+        copy.wait_send()
+    for copy in rs_copies.values():
+        copy.wait_send()
+    for h, k, copy in ag_copies:
+        copy.wait_send()
 
 
 def store_kernel(normed_ref, merged_ref, normed_hbm, merged_hbm, sem):
@@ -492,23 +541,26 @@
             pltpu.VMEM((count, part), F32),
             pltpu.VMEM((2 * count, HEAD_SIZE), BF16),
             pltpu.VMEM((peers, 2 * count, HEAD_SIZE), BF16),
-            pltpu.VMEM((peers, 2 * count, half), BF16),
-            pltpu.VMEM((peers, 2 * count, half), BF16),
+            pltpu.VMEM((2 * peers, 2 * count, chunk), BF16),
+            pltpu.VMEM((2 * peers, 2 * count, chunk), BF16),
             pltpu.VMEM((count, 128), F32),
             pltpu.VMEM((peers, count, 128), F32),
-            pltpu.VMEM((2 * count, half), BF16),
-            pltpu.VMEM((peers, 2 * count, half), BF16),
+            pltpu.VMEM((2, 2 * count, chunk), BF16),
+            pltpu.VMEM((2 * peers, 2 * count, chunk), BF16),
             pltpu.VMEM((count, part), F32),
             pltpu.VMEM((count, part), F32),
             dma((9,)),
-            dma((peers,)),
-            dma((peers,)),
-            dma((n,)),
-            dma((n,)),
-            dma((2 * n,)),
-            dma((2 * n,)),
+            dma((n, PIECES)),
+            dma((peers, PIECES)),
+            dma((n, PIECES)),
+            dma((n, PIECES)),
+            dma((2 * n, PIECES)),
+            dma((2 * n, PIECES)),
         ]
-        + [dma((peers,))] * 10,
+        + [dma((peers,))] * 4
+        + [dma((2 * peers,))] * 2
+        + [dma((peers,))] * 2
+        + [dma((2 * peers,))] * 2,
         compiler_params=pltpu.CompilerParams(
             collective_id=0, has_side_effects=True, vmem_limit_bytes=16 * 2**20
         ),

time: 23.9 us -> 23.5 us (0.983)
  Pallas kernels: 23.1 us -> 22.7 us
    pallas_call x1, Pallas kernels: 21.7 us -> 21.3 us  [fused(): pl.pallas_call(functools.partial(fused_kernel, (rows, steps, span, width,...]
where the time goes in v3:
time: 23.5 us; the launch traced here: 23.3 us
  Pallas kernels  22.7 us (97%)
  between operations  0.64 us (3%)
    pallas_call x1, Pallas kernels, fused(): pl.pallas_call(functools.partial(fused_kernel, (rows, steps, span, width,...  21.3 us
    pallas_call x1, Pallas kernels, fused(): pl.pallas_call(store_kernel, out_shape=(jax.ShapeDtypeStruct(normed.shape...  1.42 us

profile of v3, /device:TPU:0, one launch (start us, length us, event | category | flops | bytes accessed | tf_op | source)
XLA Modules:
  0.0 23.3 jit_solution(7289712621631975247)
XLA Ops:
  0.6 21.3 %shard_map.104 = (bf16[4,2,8192]{2,1,0:T(2,128)(2,1)S(1)}, bf16[128,8192]{1,0:T(8,128)(2,1)S(1)}) custom-call(s32[4]{0:T(128)} %lengths_hbm.1, bf16[4,2,8192]{2,1,0:T(2,128)(2,1)} %hidden_hbm.1, bf16[4,2,128]{2,1,0:T(2,128)(2,1)} %query_hbm.1, bf16[4,2,256]{2,1,0:T(2,128)(2,1)} %bitcast.7, bf16[4,256,256]{2,1,0:T(8,128)(2,1)} %bitcast.4, ...), custom_call_target="tpu_custom_call" | custom-call | flops 150994944 | bytes 6291456 | tf_op jit(solution)/shard_map/pallas_call | solution.py:521
  21.9 1.4 %shard_map.105 = (bf16[4,2,8192]{2,1,0:T(2,128)(2,1)}, bf16[128,8192]{1,0:T(8,128)(2,1)}) custom-call(bf16[4,2,8192]{2,1,0:T(2,128)(2,1)S(1)} %get-tuple-element.4.normed_ref, bf16[128,8192]{1,0:T(8,128)(2,1)S(1)} %get-tuple-element.5.merged_ref), custom_call_target="tpu_custom_call" | custom-call | tf_op jit(solution)/shard_map/pallas_call | solution.py:586
